TPU v7x, 32 devices: a whole 2x2x4 slice. The times are simulated.
32 devices in a mesh: row: 8 (over z, x), col: 2 (over core), vec: 2 (over y).
Axes of the slice: x: 2, y: 2, z: 4, core: 2. Of those that a mesh axis runs over, the one named last changes fastest.
Arguments:
- vectors: bfloat16 [131072, 256], P(('row', 'col'), 'vec'), parts along dimension 1, may hold values from -6 to 6
- tile_blocks: bfloat16 [8, 2, 32, 256, 256], P('row', 'col'), may hold values from -0.375 to 0.375
- block_rows: int32 [8, 2, 32], P('row', 'col'), may hold values from 0 to 63, as said below
- block_cols: int32 [8, 2, 32], P('row', 'col'), may hold values from 0 to 255, as said below
- counts: int32 [8, 2], P('row', 'col'), may hold values from 1 to 32, as said below
Outputs:
- filtered: bfloat16 [131072, 256], P(('row', 'col'), 'vec'), parts along dimension 1
There are 2 independent parts, one for each index of `vec`. A program takes and returns all parts, laid end to end along the dimension named above; an argument that names none is the same for every part. Nothing has to cross between parts.
Inputs may be any that keep to these rules, and one draw needn't show every extreme that they name: The pairs (block_rows, block_cols // 32) of the 32 slots of one tile are all distinct. Within one tile, all slots whose block columns lie in the same group of 32 (same block_cols // 32) name the same block column. `counts`: some tile uses all 32 slots.
All inputs are finite; a program needn't handle non-finite values.
Results may differ from a plain program's by a relative error of at most 0.015.
Values may be sent and summed in bfloat16 or wider, within the bound.
No kernel may reach another device: no remote copies, remote signals or barrier semaphores. Data moves between devices by JAX's collectives and lax.ppermute only.
A program may use at most 64 MiB of HBM per device.

v0:
```python
import functools

import jax
import jax.numpy as jnp
from jax import lax
from jax.experimental import pallas as pl
from jax.experimental.pallas import tpu as pltpu
from jax.sharding import PartitionSpec as P

DEGREE = 3

center_value = 0.5
half_width = 2.0

VMEM = pltpu.VMEM
SMEM = pltpu.SMEM
HBM = pltpu.HBM
DMA = pltpu.SemaphoreType.DMA
LANES = 128
FEW = 4
MANY = 4
HEAD = 8
STRIDE = 4
FIRST = 1
LAST = 2


def spec(space):
    return pl.BlockSpec(memory_space=space)


def params(mib):
    return pltpu.CompilerParams(vmem_limit_bytes=mib * 1024 * 1024)


def round_up(n, step):
    return (n + step - 1) // step * step


def plan_kernel(
    n_row,
    piece_blocks,
    sent_at,
    load_at,
    bare_at,
    place,
    wanted_a,
    wanted_b,
    meta_a,
    meta_b,
    own,
    other,
    out,
    seen,
    sems,
):
    slot_count = (meta_a.shape[0] - 1) // 2
    size = own.shape[0]

    def scan(base, own_half, meta, asked_own, asked_other, at, sent, load):
        def step(s, carry):
            at, sent, load = carry
            half = meta[s] // piece_blocks
            row = meta[s] - half * piece_blocks
            inside = half == own_half
            piece = meta[slot_count + s] // piece_blocks
            kept = jnp.where(inside, row, piece_blocks)
            entry = HEAD + STRIDE * at
            out[base + entry] = s
            out[base + entry + 1] = row
            out[base + entry + 2] = piece
            out[base + entry + 3] = jnp.where(seen[kept] == 0, FIRST, 0)
            seen[kept] = entry
            out[base + load_at + load] = s
            side = jnp.where(inside, 0, 1)
            before = sent
            for k in range(n_row):
                out[base + sent_at + STRIDE * sent] = load
                out[base + sent_at + STRIDE * sent + 1] = 2 * k + side
                out[base + sent_at + STRIDE * sent + 2] = piece
                asked = jnp.where(inside, asked_own[k, 0], asked_other[k, 0])
                sent = sent + (asked == row).astype(jnp.int32)
            return at + inside.astype(jnp.int32), sent, load + (sent > before).astype(jnp.int32)

        at, sent, load = lax.fori_loop(0, meta[2 * slot_count], step, (at, sent, load))
        for _ in range(MANY):
            for start, end, spare in ((HEAD, at, piece_blocks), (sent_at, sent, 2 * n_row)):
                entry = base + start + STRIDE * end
                out[entry] = 0
                out[entry + 1] = spare
                out[entry + 2] = 0
                out[entry + 3] = 0
            at = at + jnp.where(at % MANY == 0, 0, 1)
            sent = sent + jnp.where(sent % FEW == 0, 0, 1)
        return at, sent, load

    def lists(base, own_half, meta_own, meta_other, asked_own, asked_other):
        for b in range(piece_blocks + 1):
            seen[b] = 0
        ends = (jnp.int32(0),) * 3
        for tile, meta in enumerate((meta_own, meta_other)):
            ends = scan(base, own_half, meta, asked_own, asked_other, *ends)
            for i, end in enumerate(ends):
                out[base + 2 * i + tile] = end

        def close(b, bare):
            entry = seen[b]
            out[base + bare_at + bare] = b

            @pl.when(entry > 0)
            def _():
                out[base + entry + 3] = out[base + entry + 3] + LAST

            return bare + jnp.where(entry == 0, 1, 0)

        out[base + 6] = lax.fori_loop(0, piece_blocks, close, jnp.int32(0))
        out[base + 7] = own_half

    @pl.when(place[1] == 0)
    def _():
        lists(0, 0, meta_a, meta_b, wanted_a, wanted_b)
        copy = pltpu.make_async_copy(out.at[pl.ds(0, size)], own, sems.at[0])
        copy.start()
        lists(size, 1, meta_b, meta_a, wanted_b, wanted_a)
        handed = pltpu.make_async_copy(out.at[pl.ds(size, size)], other, sems.at[1])
        handed.start()
        copy.wait()
        handed.wait()


def settle_kernel(place, own, handed, out, sem):
    for half, source in enumerate((own, handed)):

        @pl.when(place[1] == half)
        def _():
            copy = pltpu.make_async_copy(source, out, sem)
            copy.start()
            copy.wait()


def pick_kernel(n_row, block_size, wanted, vectors, out, sems):
    def fetch(k):
        at = pl.multiple_of(wanted[k, 0] * block_size, block_size)
        return pltpu.make_async_copy(vectors.at[pl.ds(at, block_size)], out.at[k], sems.at[k])

    for k in range(n_row):
        fetch(k).start()
    for k in range(n_row):
        fetch(k).wait()


def pack_kernel(place, picked, picked_b, out, held, sems):
    n_row, _, width = picked.shape
    middle = width // 2

    def put(k):
        return pltpu.make_async_copy(held.at[k], out.at[k], sems.at[k])

    for half in range(2):

        @pl.when(place[1] == half)
        def _():
            part = slice(half * middle, (half + 1) * middle)
            for k in range(n_row):
                held[k] = jnp.concatenate([picked[k, :, part], picked_b[k, :, part]], axis=1)
                put(k).start()

    for k in range(n_row):
        put(k).wait()


def load_kernel(base, stride, ends, plan, tile_a, tile_b, blocks, sems):
    mid, end = plan[ends], plan[ends + 1]

    def copy(tile, i):
        slot = plan[base + stride * i]
        return pltpu.make_async_copy(tile.at[slot], blocks.at[i], sems.at[i])

    @pl.loop(0, mid)
    def _(i):
        copy(tile_a, i).start()

    @pl.loop(mid, end)
    def _(i):
        copy(tile_b, i).start()

    @pl.loop(0, end)
    def _(i):
        copy(tile_a, i).wait()


def load_both_kernel(base, stride, ends, plan, tile_a, tile_b, array, blocks, held, sems, held_sem):
    copy = pltpu.make_async_copy(array, held, held_sem)
    copy.start()
    load_kernel(base, stride, ends, plan, tile_a, tile_b, blocks, sems)
    copy.wait()


def each_product(plan, base, ends, blocks, pieces, use, then=None):
    mid, end = plan[ends], plan[ends + 1]
    unroll = MANY if base == HEAD else FEW

    def run(piece_ref, begin, end):
        @pl.loop(begin // unroll, end // unroll)
        def _(j):
            for u in range(unroll):
                i = unroll * j + u
                entry = base + STRIDE * i
                block = blocks[i if base == HEAD else plan[entry]]
                use(
                    entry,
                    jnp.dot(block, piece_ref[plan[entry + 2]], preferred_element_type=jnp.float32),
                )
            if then is not None:
                for u in range(unroll):
                    then(base + STRIDE * (unroll * j + u))

    run(pieces[0], 0, mid)
    run(pieces[1], mid, end)


def add_products(plan, base, ends, blocks, pieces, total):
    def use(entry, value):
        total[plan[entry + 1]] += value

    each_product(plan, base, ends, blocks, pieces, use)


def split_sides(pieces, vec):
    middle = vec.shape[-1] // 2
    column = lax.broadcasted_iota(jnp.int32, (1, vec.shape[-1]), 1)
    for side in range(2):
        keep = jnp.where((column // middle) == side, 1.0, 0.0).astype(jnp.bfloat16)
        for p in range(vec.shape[1]):
            vec[side, p] = pieces[p] * keep


def joined(total, k):
    one, two = total[2 * k], total[2 * k + 1]
    low = lax.broadcasted_iota(jnp.int32, one.shape, 1) < one.shape[1] // 2
    return jnp.where(low, one, two) + pltpu.roll(
        jnp.where(low, two, one), one.shape[1] // 2, axis=1
    )


def first_sent_kernel(
    sent_at, load_at, plan, tile_a, tile_b, pieces, start, out, blocks, vec, total, held, held_sem, sems
):
    n_row = out.shape[0]
    mid, end = plan[4], plan[5]

    def fetch(tile, i):
        return pltpu.make_async_copy(tile.at[plan[load_at + i]], blocks.at[i], sems.at[i])

    @pl.loop(0, mid)
    def _(i):
        fetch(tile_a, i).start()

    @pl.loop(mid, end)
    def _(i):
        fetch(tile_b, i).start()

    copy = pltpu.make_async_copy(start, held, held_sem)
    copy.start()
    split_sides(pieces, vec)
    total[...] = jnp.zeros_like(total)

    @pl.loop(0, end)
    def _(i):
        fetch(tile_a, i).wait()

    add_products(plan, sent_at, 2, blocks, (vec.at[0], vec.at[1]), total)
    copy.wait()
    for k in range(n_row):
        value = joined(total, k) - center_value * held[k].astype(jnp.float32)
        out[k] = (value / half_width).astype(jnp.bfloat16)


def second_sent_kernel(
    sent_at, plan, blocks, pieces, current, previous, out, vec, total, held, held_sem, ready, out_sems
):
    n_row = out.shape[0]
    copy = pltpu.make_async_copy(previous, held, held_sem)
    copy.start()
    split_sides(pieces, vec)
    total[...] = jnp.zeros_like(total)
    add_products(plan, sent_at, 2, blocks, (vec.at[0], vec.at[1]), total)
    copy.wait()

    def put(k):
        return pltpu.make_async_copy(ready.at[k], out.at[k], out_sems.at[k])

    for k in range(n_row):
        value = joined(total, k) - center_value * current[k].astype(jnp.float32)
        ready[k] = (value - held[k].astype(jnp.float32)).astype(jnp.bfloat16)
        put(k).start()
    for k in range(n_row):
        put(k).wait()


def whole_columns(half, mine, other, vec, at):
    n_row, _, width = mine.shape
    middle = width // 2

    @pl.when(half == 0)
    def _():
        @pl.loop(0, n_row)
        def _(p):
            one, two = mine[p], other[p]
            vec[0, p, :, at : at + width] = jnp.concatenate([one[:, :middle], two[:, middle:]], axis=1)
            vec[1, p, :, at : at + width] = jnp.concatenate([one[:, middle:], two[:, :middle]], axis=1)

    @pl.when(half != 0)
    def _():
        @pl.loop(0, n_row)
        def _(p):
            one, two = mine[p], other[p]
            vec[0, p, :, at : at + width] = jnp.concatenate([two[:, middle:], one[:, :middle]], axis=1)
            vec[1, p, :, at : at + width] = jnp.concatenate([two[:, :middle], one[:, middle:]], axis=1)


def early_kernel(plan, blocks, q1, q1_other, q2, q2_other, vectors, base, vec, total, own, sem, row_sems):
    width = vectors.shape[1]
    piece_blocks, block_size, _ = base.shape
    copy = pltpu.make_async_copy(vectors, own, sem)
    copy.start()
    whole_columns(plan[7], q1, q1_other, vec, 0)
    whole_columns(plan[7], q2, q2_other, vec, width)
    copy.wait()

    def rows(b):
        return pl.ds(pl.multiple_of(b * block_size, block_size), block_size)

    def put(b):
        return pltpu.make_async_copy(own.at[rows(b)], base.at[b], row_sems.at[b])

    @pl.loop(0, piece_blocks)
    def _(b):
        value = own[rows(b), :].astype(jnp.float32)
        total[b, :, :width] = -center_value * value
        total[b, :, width:] = -value

    add_products(plan, HEAD, 0, blocks, (vec.at[0], vec.at[1]), total)

    @pl.loop(0, piece_blocks)
    def _(b):
        first = (total[b, :, :width] / half_width).astype(jnp.bfloat16).astype(jnp.float32)
        second = total[b, :, width:] - center_value * first
        second = second.astype(jnp.bfloat16).astype(jnp.float32)
        own[rows(b), :] = (-center_value * second - first).astype(jnp.bfloat16)
        put(b).start()

    @pl.loop(0, piece_blocks)
    def _(b):
        put(b).wait()


def last_kernel(bare_at, plan, blocks, mine, other, base, out, vec, total, own, row_sems):
    piece_blocks = base.shape[0]

    def put(source, b):
        return pltpu.make_async_copy(source.at[b], out.at[b], row_sems.at[b])

    @pl.loop(0, plan[6])
    def _(i):
        b = plan[bare_at + i]
        put(base, b).start()

    whole_columns(plan[7], mine, other, vec, 0)

    def use(entry, value):
        row = plan[entry + 1]
        marks = plan[entry + 3]
        start = base[jnp.minimum(row, piece_blocks - 1)].astype(jnp.float32)
        value = jnp.where(lax.rem(marks, LAST) == FIRST, start, total[row]) + value
        total[row] = value
        own[row] = value.astype(jnp.bfloat16)

    def then(entry):
        @pl.when(plan[entry + 3] >= LAST)
        def _():
            put(own, plan[entry + 1]).start()

    each_product(plan, HEAD, 0, blocks, (vec.at[0], vec.at[1]), use, then)

    @pl.loop(0, piece_blocks)
    def _(b):
        put(own, b).wait()


def after(value, *others):
    return lax.optimization_barrier((value, *others))[0]


def call(kernel, out, args, spaces, scratch, mib, name, estimate=None):
    args = [
        pltpu.with_memory_space_constraint(arg, space) if space in (VMEM, HBM) or tied else arg
        for arg, (space, tied) in zip(args, spaces)
    ]
    return pl.pallas_call(
        kernel,
        out_shape=[space(shape, dtype) for shape, dtype, space in out],
        in_specs=[spec(space) for space, _ in spaces],
        out_specs=[spec(space) for _, _, space in out],
        scratch_shapes=scratch,
        compiler_params=params(mib),
        cost_estimate=estimate,
        name=name,
    )(*args)


HERE = (VMEM, True)
FAR = (HBM, True)
LIST = (SMEM, True)
SCALARS = (SMEM, False)
ANYWHERE = (pl.ANY, False)


def on_pair(vectors, tile_blocks, block_rows, block_cols, counts):
    n_row = lax.axis_size("row")
    tile = tile_blocks[0, 0]
    slot_rows = block_rows[0, 0]
    slot_cols = block_cols[0, 0]
    used = counts[0]
    slot_count, block_size, _ = tile.shape
    width = vectors.shape[1]
    piece_blocks = vectors.shape[0] // block_size
    place = jnp.stack([lax.axis_index("row"), lax.axis_index("col")]).astype(jnp.int32)

    across = functools.partial(lax.ppermute, axis_name="col", perm=[(0, 1), (1, 0)])

    needed = jnp.max(
        jnp.where(
            slot_cols[None, :] // piece_blocks == jnp.arange(n_row)[:, None],
            slot_cols[None, :] % piece_blocks,
            0,
        ),
        axis=1,
        keepdims=True,
    )
    exchange = functools.partial(
        lax.all_to_all, axis_name="row", split_axis=0, concat_axis=0, tiled=True
    )
    meta = jnp.concatenate([slot_rows, slot_cols, used])
    meta_other = across(meta)
    wanted = after(exchange(jnp.broadcast_to(needed, (n_row, LANES))), meta_other, place)
    sent_shape = (n_row, block_size, width)
    (sent,) = call(
        functools.partial(pick_kernel, n_row, block_size),
        [(sent_shape, jnp.bfloat16, VMEM)],
        (wanted, vectors),
        (SCALARS, FAR),
        [DMA((n_row,))],
        2,
        "pick",
    )
    tile_other = across(tile)
    sent_other = across(sent)
    wanted_other = across(after(wanted, sent))
    packed = call(
        pack_kernel,
        [(sent_shape, jnp.bfloat16, HBM)],
        (place, sent, sent_other),
        (SCALARS, HERE, HERE),
        [VMEM(sent_shape, jnp.bfloat16), DMA((n_row,))],
        4,
        "pack",
    )[0]

    capacity = 2 * round_up(slot_count, MANY)
    sent_at = HEAD + STRIDE * (capacity + 1)
    load_at = sent_at + STRIDE * (4 * n_row * n_row + 2 * FEW + 1)
    bare_at = load_at + 2 * slot_count + 1
    plan_size = round_up(bare_at + piece_blocks, 8 * LANES)
    own_list, other_list = call(
        functools.partial(plan_kernel, n_row, piece_blocks, sent_at, load_at, bare_at),
        [((plan_size,), jnp.int32, HBM)] * 2,
        (place, wanted, wanted_other, meta, meta_other),
        (SCALARS,) * 5,
        [SMEM((2 * plan_size,), jnp.int32), SMEM((piece_blocks + 1,), jnp.int32), DMA((2,))],
        2,
        "plan",
    )
    q1 = exchange(after(packed, own_list))
    plan = call(
        settle_kernel,
        [((plan_size,), jnp.int32, SMEM)],
        (place, own_list, across(after(other_list, packed))),
        (SCALARS, ANYWHERE, ANYWHERE),
        [DMA],
        2,
        "settle",
    )[0]

    def load(base, stride, ends, cue, *array):
        kernel = load_both_kernel if array else load_kernel
        return call(
            functools.partial(kernel, base, stride, ends),
            [((capacity, block_size, block_size), jnp.bfloat16, VMEM)]
            + [(held.shape, held.dtype, VMEM) for held in array],
            (after(plan, cue), tile, tile_other, *array),
            (LIST, FAR, ANYWHERE) + (FAR,) * len(array),
            [DMA((capacity,))] + [DMA] * len(array),
            2,
            "load",
        )

    def cost(products, rows):
        size = block_size * width
        return pl.CostEstimate(
            flops=2 * products * block_size * size,
            bytes_accessed=2 * (products * block_size * block_size + 3 * rows * size),
            transcendentals=0,
        )

    sums = [
        VMEM((2, n_row, block_size, width), jnp.bfloat16),
        VMEM((2 * n_row + 1, block_size, width), jnp.float32),
    ]

    def first_blocks(*args):
        return call(
            functools.partial(first_sent_kernel, sent_at, load_at),
            [
                (sent_shape, jnp.bfloat16, VMEM),
                ((capacity, block_size, block_size), jnp.bfloat16, VMEM),
            ],
            (plan, tile, tile_other, *args),
            (LIST, FAR, ANYWHERE, HERE, FAR),
            sums + [VMEM(sent_shape, jnp.bfloat16), DMA, DMA((capacity,))],
            8,
            "sent",
            cost(n_row, n_row),
        )

    def second_blocks(*args):
        return call(
            functools.partial(second_sent_kernel, sent_at),
            [(sent_shape, jnp.bfloat16, HBM)],
            (plan, *args),
            (LIST, HERE, HERE, HERE, FAR),
            sums
            + [VMEM(sent_shape, jnp.bfloat16), DMA, VMEM(sent_shape, jnp.bfloat16), DMA((n_row,))],
            8,
            "sent",
            cost(n_row, n_row),
        )[0]

    base_shape = (piece_blocks, block_size, width)

    def early(*args):
        return call(
            early_kernel,
            [(base_shape, jnp.bfloat16, HBM)],
            (plan, *args),
            (LIST, HERE, HERE, HERE, HERE, HERE, FAR),
            [
                VMEM((2, n_row, block_size, 2 * width), jnp.bfloat16),
                VMEM((piece_blocks + 1, block_size, 2 * width), jnp.float32),
                VMEM(vectors.shape, jnp.bfloat16),
                DMA,
                DMA((piece_blocks,)),
            ],
            18,
            "early",
            cost(2 * slot_count, 2 * piece_blocks),
        )[0]

    def last(blocks, *args):
        rows = (piece_blocks + 1, block_size, width)
        (out,) = call(
            functools.partial(last_kernel, bare_at),
            [(base_shape, jnp.bfloat16, HBM)],
            (plan, blocks, *args),
            (LIST,) + (HERE,) * 4,
            [
                VMEM((2, n_row, block_size, width), jnp.bfloat16),
                VMEM(rows, jnp.float32),
                VMEM(rows, jnp.bfloat16),
                DMA((piece_blocks,)),
            ],
            9,
            "last",
            cost(slot_count, piece_blocks),
        )
        return out.reshape(vectors.shape)

    q1 = after(q1, plan)
    first_sent, blocks = first_blocks(q1, packed)
    q2 = exchange(first_sent)
    second_sent = second_blocks(blocks, q2, first_sent, packed)
    q1_other = across(after(q1, second_sent))
    q2_other = across(after(q2, second_sent))
    (blocks,) = load(HEAD, STRIDE, 0, second_sent)
    base = early(blocks, q1, q1_other, q2, q2_other, vectors)
    q3 = after(exchange(second_sent), base)
    q3_other = across(q3)
    blocks, base = load(HEAD, STRIDE, 0, q3, base)
    return last(blocks, q3, q3_other, base)


def on_any(vectors, tile_blocks, block_rows, block_cols, counts):
    n_row = lax.axis_size("row")
    n_col = lax.axis_size("col")
    tile_data = tile_blocks[0, 0]
    slot_rows = block_rows[0, 0]
    slot_cols = block_cols[0, 0]
    used = counts[0, 0]
    block_size = tile_data.shape[-1]
    width = vectors.shape[1]
    piece_blocks = vectors.shape[0] // block_size
    row_blocks = piece_blocks * n_col
    slot_count = tile_data.shape[0]
    live = (jnp.arange(slot_count) < used).astype(jnp.float32)
    onehot = (slot_rows[None, :] == jnp.arange(row_blocks)[:, None]).astype(jnp.float32) * live[
        None, :
    ]
    source_piece = slot_cols // piece_blocks
    offset = slot_cols % piece_blocks
    needed = jnp.max(
        jnp.where(source_piece[None, :] == jnp.arange(n_row)[:, None], offset[None, :], 0), axis=1
    )
    wanted = lax.all_to_all(
        needed.reshape(n_row, 1), "row", split_axis=0, concat_axis=0, tiled=True
    ).reshape(n_row)

    def apply_tiles(current):
        own_blocks = current.reshape(piece_blocks, block_size, width)
        outgoing = jnp.take(own_blocks, wanted, axis=0)
        received = lax.all_to_all(outgoing, "row", split_axis=0, concat_axis=0, tiled=True)
        vec_blocks = jnp.take(received, source_piece, axis=0)
        products = jnp.einsum(
            "sij,sjk->sik", tile_data, vec_blocks, preferred_element_type=jnp.float32
        )
        term = jnp.einsum("ls,sik->lik", onehot, products, precision=lax.Precision.HIGHEST)
        term = term.reshape(row_blocks * block_size, width)
        return lax.psum_scatter(
            term.astype(jnp.bfloat16), "col", scatter_dimension=0, tiled=True
        ).astype(jnp.float32)

    previous = vectors
    applied = apply_tiles(vectors)
    current = ((applied - center_value * previous.astype(jnp.float32)) / half_width).astype(
        jnp.bfloat16
    )
    for repeat in range(DEGREE - 1):
        applied = apply_tiles(current)
        following = (
            2.0 * (applied - center_value * current.astype(jnp.float32)) / half_width
            - previous.astype(jnp.float32)
        ).astype(jnp.bfloat16)
        previous, current = (current, following)
    return current


def solution(mesh):
    n_row, n_col = mesh.shape["row"], mesh.shape["col"]
    paired = n_col == 2 and n_row & (n_row - 1) == 0
    return jax.shard_map(
        on_pair if paired else on_any,
        mesh=mesh,
        in_specs=(
            P(("row", "col"), "vec"),
            P("row", "col", None, None, None),
            P("row", "col", None),
            P("row", "col", None),
            P("row", "col"),
        ),
        out_specs=P(("row", "col"), "vec"),
        check_vma=False,
    )
```

profile of v0, /device:TPU:0, one launch (start us, length us, event | category | flops | bytes accessed | tf_op | source)
XLA Modules:
  0.0 86.5 jit_solution(4548849570023114032)
XLA Ops:
  0.5 0.7 and_select_fusion.1
  1.2 0.7 broadcast_in_dim.21
  1.9 6.8 %all-to-all-start = ((s32[8,1,128]{2,1,0:T(1,128)}), s32[8,1,128]{2,1,0:T(1,128)S(1)}, u32[]{:S(2)}, u32[]{:S(2)}) async-start(s32[8,1,128]{2,1,0:T(1,128)} %broadcast_in_dim.21), calls=%async_computation | async-start | bytes 8192 | tf_op jit(solution)/shard_map/all_to_all | solution.py:446
  9.4 0.7 pad_add_fusion.1.meta_a
  10.4 0.8 collective-permute-done.meta_b
  11.2 3.9 %all-to-all-done = s32[8,1,128]{2,1,0:T(1,128)S(1)} async-done(((s32[8,1,128]{2,1,0:T(1,128)}), s32[8,1,128]{2,1,0:T(1,128)S(1)}, u32[]{:S(2)}, u32[]{:S(2)}) %all-to-all-start) | async-done | bytes 4128 | tf_op jit(solution)/shard_map/all_to_all | solution.py:446
  15.1 1.7 %pick.1.picked = bf16[8,256,128]{2,1,0:T(8,128)(2,1)S(1)} custom-call(s32[8,128]{1,0:T(8,128)S(1)} %bitcast.15, bf16[8192,128]{1,0:T(8,128)(2,1)} %vectors.3), custom_call_target="tpu_custom_call" | custom-call | tf_op jit(solution)/shard_map/pick/pallas_call | solution.py:400
  17.4 1.4 %collective-permute-done.1.wanted_b = s32[8,128]{1,0:T(8,128)S(1)} collective-permute-done((s32[8,128]{1,0:T(8,128)S(1)}, s32[8,128]{1,0:T(8,128)S(1)}, u32[]{:S(2)}, u32[]{:S(2)}) %collective-permute-start.1) | collective-permute-done | bytes 4128 | tf_op jit(solution)/shard_map/ppermute | solution.py:459
  18.8 9.4 %plan.1 = (s32[2048]{0:T(1024)}, s32[2048]{0:T(1024)}) custom-call(s32[2]{0:T(128)S(1)} %pad_add_fusion.place, s32[8,128]{1,0:T(8,128)S(1)} %bitcast.17, s32[8,128]{1,0:T(8,128)S(1)} %collective-permute-done.1.wanted_b, s32[65]{0:T(128)S(1)} %pad_add_fusion.1.meta_a, s32[65]{0:T(128)S(1)} %collective-permute-done.meta_b), custom_call_target="tpu_custom_call" | custom-call | tf_op jit(solution)/shard_map/plan/pallas_call | solution.py:400
  28.3 1.5 %pack.1.start.previous = bf16[8,256,128]{2,1,0:T(8,128)(2,1)} custom-call(s32[2]{0:T(128)S(1)} %pad_add_fusion.place, bf16[8,256,128]{2,1,0:T(8,128)(2,1)S(1)} %pick.1.picked, bf16[8,256,128]{2,1,0:T(8,128)(2,1)S(1)} %collective-permute-done.2.picked_b), custom_call_target="tpu_custom_call" | custom-call | tf_op jit(solution)/shard_map/pack/pallas_call | solution.py:400
  29.8 3.5 %all-to-all-start.1 = ((bf16[8,256,128]{2,1,0:T(8,128)(2,1)}), bf16[8,256,128]{2,1,0:T(8,128)(2,1)S(1)}, u32[]{:S(2)}, u32[]{:S(2)}) async-start(bf16[8,256,128]{2,1,0:T(8,128)(2,1)} %pack.1.start.previous), calls=%async_computation.1 | async-start | bytes 1048576 | tf_op jit(solution)/shard_map/all_to_all | solution.py:484
  33.4 1.4 %collective-permute-done.3.handed = s32[2048]{0:T(1024)S(1)} collective-permute-done((s32[2048]{0:T(1024)}, s32[2048]{0:T(1024)S(1)}, u32[]{:S(2)}, u32[]{:S(2)}) %collective-permute-start.3) | collective-permute-done | bytes 8224 | tf_op jit(solution)/shard_map/ppermute | solution.py:488
  34.7 0.7 copy-done
  35.4 1.2 %settle.1.plan = s32[2048]{0:T(1024)S(4)} custom-call(s32[2]{0:T(128)S(1)} %pad_add_fusion.place, s32[2048]{0:T(1024)S(1)} %copy-done, s32[2048]{0:T(1024)S(1)} %collective-permute-done.3.handed), custom_call_target="tpu_custom_call" | custom-call | tf_op jit(solution)/shard_map/settle/pallas_call | solution.py:400
  36.7 6.8 %all-to-all-done.1.pieces.q1 = bf16[8,256,128]{2,1,0:T(8,128)(2,1)S(1)} async-done(((bf16[8,256,128]{2,1,0:T(8,128)(2,1)}), bf16[8,256,128]{2,1,0:T(8,128)(2,1)S(1)}, u32[]{:S(2)}, u32[]{:S(2)}) %all-to-all-start.1) | async-done | bytes 524320 | tf_op jit(solution)/shard_map/all_to_all | solution.py:484
  43.5 3.6 %sent.2 = (bf16[8,256,128]{2,1,0:T(8,128)(2,1)S(1)}, bf16[64,256,256]{2,1,0:T(8,128)(2,1)S(1)}) custom-call(s32[2048]{0:T(1024)S(4)} %settle.1.plan, bf16[32,256,256]{2,1,0:T(8,128)(2,1)} %bitcast.19, bf16[32,256,256]{2,1,0:T(8,128)(2,1)} %collective-permute-done.4.tile_b, bf16[8,256,128]{2,1,0:T(8,128)(2,1)S(1)} %all-to-all-done.1.pieces.q1, ...), custom_call_target="tpu_custom_call" | custom-call | flops 134217728 | bytes 2621440 | tf_op jit(solution)/shard_map/sent/pallas_call | solution.py:400
  47.1 13.5 %all_to_all.24.pieces.q2 = bf16[8,256,128]{2,1,0:T(8,128)(2,1)S(1)} all-to-all(bf16[8,256,128]{2,1,0:T(8,128)(2,1)S(1)} %get-tuple-element.29.current), channel_id=1, replica_groups=mesh['row'=8,'col'=2,'vec'=2] {'row'}, dimensions={0} | all-to-all | bytes 1048576 | tf_op jit(solution)/shard_map/all_to_all | solution.py:590
  60.6 2.5 %sent.3 = bf16[8,256,128]{2,1,0:T(8,128)(2,1)} custom-call(s32[2048]{0:T(1024)S(4)} %settle.1.plan, bf16[64,256,256]{2,1,0:T(8,128)(2,1)S(1)} %get-tuple-element.28.blocks, bf16[8,256,128]{2,1,0:T(8,128)(2,1)S(1)} %all_to_all.24.pieces.q2, bf16[8,256,128]{2,1,0:T(8,128)(2,1)S(1)} %get-tuple-element.29.current, bf16[8,256,128]{2,1,0:T(8,128)(2,1)} %pack.1.start.previous), custom_call_target="tpu_custom_call" | custom-call | flops 134217728 | bytes 2621440 | tf_op jit(solution)/shard_map/sent/pallas_call | solution.py:400
  63.1 3.5 %all-to-all-start.3 = ((bf16[8,256,128]{2,1,0:T(8,128)(2,1)}), bf16[8,256,128]{2,1,0:T(8,128)(2,1)S(1)}, u32[]{:S(2)}, u32[]{:S(2)}) async-start(bf16[8,256,128]{2,1,0:T(8,128)(2,1)} %sent.3), calls=%async_computation.3 | async-start | bytes 1048576 | tf_op jit(solution)/shard_map/all_to_all | solution.py:596
  67.2 2.7 %load.2.blocks = bf16[64,256,256]{2,1,0:T(8,128)(2,1)S(1)} custom-call(s32[2048]{0:T(1024)S(4)} %settle.1.plan, bf16[32,256,256]{2,1,0:T(8,128)(2,1)} %bitcast.20, bf16[32,256,256]{2,1,0:T(8,128)(2,1)} %collective-permute-done.4.tile_b), custom_call_target="tpu_custom_call" | custom-call | tf_op jit(solution)/shard_map/load/pallas_call | solution.py:400
  69.9 7.0 %early.1.array = bf16[32,256,128]{2,1,0:T(8,128)(2,1)} custom-call(s32[2048]{0:T(1024)S(4)} %settle.1.plan, bf16[64,256,256]{2,1,0:T(8,128)(2,1)S(1)} %load.2.blocks, bf16[8,256,128]{2,1,0:T(8,128)(2,1)S(1)} %all-to-all-done.1.pieces.q1, bf16[8,256,128]{2,1,0:T(8,128)(2,1)S(1)} %collective-permute-done.5.q1_other, ...), custom_call_target="tpu_custom_call" | custom-call | flops 1073741824 | bytes 20971520 | tf_op jit(solution)/shard_map/early/pallas_call | solution.py:400
  76.9 2.1 %all-to-all-done.3.mine = bf16[8,256,128]{2,1,0:T(8,128)(2,1)S(1)} async-done(((bf16[8,256,128]{2,1,0:T(8,128)(2,1)}), bf16[8,256,128]{2,1,0:T(8,128)(2,1)S(1)}, u32[]{:S(2)}, u32[]{:S(2)}) %all-to-all-start.3) | async-done | bytes 524320 | tf_op jit(solution)/shard_map/all_to_all | solution.py:596
  79.1 3.2 %load.3 = (bf16[64,256,256]{2,1,0:T(8,128)(2,1)S(1)}, bf16[32,256,128]{2,1,0:T(8,128)(2,1)S(1)}) custom-call(s32[2048]{0:T(1024)S(4)} %settle.1.plan, bf16[32,256,256]{2,1,0:T(8,128)(2,1)} %bitcast.21, bf16[32,256,256]{2,1,0:T(8,128)(2,1)} %collective-permute-done.4.tile_b, bf16[32,256,128]{2,1,0:T(8,128)(2,1)} %early.1.array), custom_call_target="tpu_custom_call" | custom-call | tf_op jit(solution)/shard_map/load/pallas_call | solution.py:400
  82.3 4.2 %last.1 = bf16[32,256,128]{2,1,0:T(8,128)(2,1)} custom-call(s32[2048]{0:T(1024)S(4)} %settle.1.plan, bf16[64,256,256]{2,1,0:T(8,128)(2,1)S(1)} %get-tuple-element.35.blocks, bf16[8,256,128]{2,1,0:T(8,128)(2,1)S(1)} %all-to-all-done.3.mine, bf16[8,256,128]{2,1,0:T(8,128)(2,1)S(1)} %collective-permute-done.7.other, ...), custom_call_target="tpu_custom_call" | custom-call | flops 536870912 | bytes 10485760 | tf_op jit(solution)/shard_map/last/pallas_call | solution.py:400
  (16 shorter events, 2.1 us)
Async XLA Ops:
  0.0 43.5 %collective-permute-start.4 = (bf16[32,256,256]{2,1,0:T(8,128)(2,1)}, bf16[32,256,256]{2,1,0:T(8,128)(2,1)}, u32[]{:S(2)}, u32[]{:S(2)}) collective-permute-start(bf16[32,256,256]{2,1,0:T(8,128)(2,1)} %bitcast.18), channel_id=1, source_target_pairs={{0,2},{2,0},{1,3},{3,1},{4,6},{6,4},{5,7},{7,5},{8,10},{10,8},{9,1... | collective-permute-start | bytes 12582920 | tf_op jit(solution)/shard_map/ppermute | solution.py:457
  1.9 13.2 %all-to-all-start = ((s32[8,1,128]{2,1,0:T(1,128)}), s32[8,1,128]{2,1,0:T(1,128)S(1)}, u32[]{:S(2)}, u32[]{:S(2)}) async-start(s32[8,1,128]{2,1,0:T(1,128)} %broadcast_in_dim.21), calls=%async_computation | async-start | bytes 8192 | tf_op jit(solution)/shard_map/all_to_all | solution.py:446
  10.1 1.1 %collective-permute-start = (s32[65]{0:T(128)S(1)}, s32[65]{0:T(128)S(1)}, u32[]{:S(2)}, u32[]{:S(2)}) collective-permute-start(s32[65]{0:T(128)S(1)} %pad_add_fusion.1.meta_a), channel_id=1, source_target_pairs={{0,2},{2,0},{1,3},{3,1},{4,6},{6,4},{5,7},{7,5},{8,10},{10,8},{9,1... | collective-permute-start | bytes 788 | tf_op jit(solution)/shard_map/ppermute | solution.py:445
  16.8 11.4 %collective-permute-start.2 = (bf16[8,256,128]{2,1,0:T(8,128)(2,1)S(1)}, bf16[8,256,128]{2,1,0:T(8,128)(2,1)S(1)}, u32[]{:S(2)}, u32[]{:S(2)}) collective-permute-start(bf16[8,256,128]{2,1,0:T(8,128)(2,1)S(1)} %pick.1.picked), channel_id=1, source_target_pairs={{0,2},{2,0},{1,3},{3,1},{4,6},{6,4},{5,7},{7,5},{8,10},{10,8},{9,1... | collective-permute-start | bytes 1572872 | tf_op jit(solution)/shard_map/ppermute | solution.py:458
  16.9 1.9 %collective-permute-start.1 = (s32[8,128]{1,0:T(8,128)S(1)}, s32[8,128]{1,0:T(8,128)S(1)}, u32[]{:S(2)}, u32[]{:S(2)}) collective-permute-start(s32[8,128]{1,0:T(8,128)S(1)} %bitcast.16), channel_id=1, source_target_pairs={{0,2},{2,0},{1,3},{3,1},{4,6},{6,4},{5,7},{7,5},{8,10},{10,8},{9,1... | collective-permute-start | bytes 12296 | tf_op jit(solution)/shard_map/ppermute | solution.py:459
  29.8 13.7 %all-to-all-start.1 = ((bf16[8,256,128]{2,1,0:T(8,128)(2,1)}), bf16[8,256,128]{2,1,0:T(8,128)(2,1)S(1)}, u32[]{:S(2)}, u32[]{:S(2)}) async-start(bf16[8,256,128]{2,1,0:T(8,128)(2,1)} %pack.1.start.previous), calls=%async_computation.1 | async-start | bytes 1048576 | tf_op jit(solution)/shard_map/all_to_all | solution.py:484
  33.3 1.4 %collective-permute-start.3 = (s32[2048]{0:T(1024)}, s32[2048]{0:T(1024)S(1)}, u32[]{:S(2)}, u32[]{:S(2)}) collective-permute-start(s32[2048]{0:T(1024)} %get-tuple-element.25), channel_id=1, source_target_pairs={{0,2},{2,0},{1,3},{3,1},{4,6},{6,4},{5,7},{7,5},{8,10},{10,8},{9,1... | collective-permute-start | bytes 24584 | tf_op jit(solution)/shard_map/ppermute | solution.py:488
  34.7 0.7 copy-start
  63.1 15.9 %all-to-all-start.3 = ((bf16[8,256,128]{2,1,0:T(8,128)(2,1)}), bf16[8,256,128]{2,1,0:T(8,128)(2,1)S(1)}, u32[]{:S(2)}, u32[]{:S(2)}) async-start(bf16[8,256,128]{2,1,0:T(8,128)(2,1)} %sent.3), calls=%async_computation.3 | async-start | bytes 1048576 | tf_op jit(solution)/shard_map/all_to_all | solution.py:596
  66.6 3.2 %collective-permute-start.6 = (bf16[8,256,128]{2,1,0:T(8,128)(2,1)S(1)}, bf16[8,256,128]{2,1,0:T(8,128)(2,1)S(1)}, u32[]{:S(2)}, u32[]{:S(2)}) collective-permute-start(bf16[8,256,128]{2,1,0:T(8,128)(2,1)S(1)} %all_to_all.24.pieces.q2), channel_id=1, source_target_pairs={{0,2},{2,0},{1,3},{3,1},{4,6},{6,4},{5,7},{7,5},{8,10},{10,8},{9,1... | collective-permute-start | bytes 1572872 | tf_op jit(solution)/shard_map/ppermute | solution.py:593
  66.7 3.2 %collective-permute-start.5 = (bf16[8,256,128]{2,1,0:T(8,128)(2,1)S(1)}, bf16[8,256,128]{2,1,0:T(8,128)(2,1)S(1)}, u32[]{:S(2)}, u32[]{:S(2)}) collective-permute-start(bf16[8,256,128]{2,1,0:T(8,128)(2,1)S(1)} %all-to-all-done.1.pieces.q1), channel_id=1, source_target_pairs={{0,2},{2,0},{1,3},{3,1},{4,6},{6,4},{5,7},{7,5},{8,10},{10,8},{9,1... | collective-permute-start | bytes 1572872 | tf_op jit(solution)/shard_map/ppermute | solution.py:592
  79.1 3.2 %collective-permute-start.7 = (bf16[8,256,128]{2,1,0:T(8,128)(2,1)S(1)}, bf16[8,256,128]{2,1,0:T(8,128)(2,1)S(1)}, u32[]{:S(2)}, u32[]{:S(2)}) collective-permute-start(bf16[8,256,128]{2,1,0:T(8,128)(2,1)S(1)} %all-to-all-done.3.mine), channel_id=1, source_target_pairs={{0,2},{2,0},{1,3},{3,1},{4,6},{6,4},{5,7},{7,5},{8,10},{10,8},{9,1... | collective-permute-start | bytes 1572872 | tf_op jit(solution)/shard_map/ppermute | solution.py:597
where the time goes:
time: 86.9 us; the launch traced here: 86.5 us
  Pallas kernels  37.1 us (43%)
  waiting for transfers between devices  16.4 us (19%)
  starting transfers between devices  15.7 us (18%)
  blocking collectives  13.5 us (16%)
  other arithmetic  1.61 us (2%)
  local copies, waits for them, and re-layouts  1.37 us (2%)
    pallas_call x10, Pallas kernels, call(): pl.pallas_call(kernel, out_shape=[space(shape, dtype) for shape, dtype, s...  37.1 us
    all_to_all x1, blocking collectives, on_pair(): q2 = exchange(first_sent)  13.5 us
    all_to_all x1, waiting for transfers between devices, on_pair(): q1 = exchange(after(packed, own_list))  6.82 us
    all_to_all x1, starting transfers between devices, on_pair(): exchange(jnp.broadcast_to(needed, (n_row, LANES)))  6.8 us
    all_to_all x1, waiting for transfers between devices, on_pair(): exchange(jnp.broadcast_to(needed, (n_row, LANES)))  3.86 us
    all_to_all x1, starting transfers between devices, on_pair(): q1 = exchange(after(packed, own_list))  3.51 us
    all_to_all x1, starting transfers between devices, on_pair(): q3 = after(exchange(second_sent), base)  3.5 us
    all_to_all x1, waiting for transfers between devices, on_pair(): q3 = after(exchange(second_sent), base)  2.13 us
  transfers between devices with their start and end apart: 11, of which 6 were waited for; matrix products, arithmetic and copies ran while one was open for 3% of the time, Pallas kernels for 31%

commit v1 on v0

--- a/solution.py
+++ b/solution.py
@@ -52,17 +52,21 @@
     other,
     out,
     seen,
+    asked,
     sems,
 ):
     slot_count = (meta_a.shape[0] - 1) // 2
     size = own.shape[0]
 
-    def scan(base, own_half, meta, asked_own, asked_other, at, sent, load):
+    def scan(base, own_half, meta, at, sent, load):
+        used = meta[2 * slot_count]
+
         def step(s, carry):
             at, sent, load = carry
             half = meta[s] // piece_blocks
             row = meta[s] - half * piece_blocks
-            inside = half == own_half
+            live = s < used
+            inside = live & (half == own_half)
             piece = meta[slot_count + s] // piece_blocks
             kept = jnp.where(inside, row, piece_blocks)
             entry = HEAD + STRIDE * at
@@ -72,17 +76,29 @@
             out[base + entry + 3] = jnp.where(seen[kept] == 0, FIRST, 0)
             seen[kept] = entry
             out[base + load_at + load] = s
-            side = jnp.where(inside, 0, 1)
-            before = sent
-            for k in range(n_row):
-                out[base + sent_at + STRIDE * sent] = load
-                out[base + sent_at + STRIDE * sent + 1] = 2 * k + side
-                out[base + sent_at + STRIDE * sent + 2] = piece
-                asked = jnp.where(inside, asked_own[k, 0], asked_other[k, 0])
-                sent = sent + (asked == row).astype(jnp.int32)
-            return at + inside.astype(jnp.int32), sent, load + (sent > before).astype(jnp.int32)
-
-        at, sent, load = lax.fori_loop(0, meta[2 * slot_count], step, (at, sent, load))
+            sought = jnp.where(live, row, -1)
+            hits = [(asked[half * n_row + k] == sought).astype(jnp.int32) for k in range(n_row)]
+            found = sum(hits)
+
+            @pl.when(found > 0)
+            def _():
+                side = jnp.where(inside, 0, 1)
+                place = sent
+                for k in range(n_row):
+                    entry = base + sent_at + STRIDE * place
+                    out[entry] = load
+                    out[entry + 1] = 2 * k + side
+                    out[entry + 2] = piece
+                    out[entry + 3] = jnp.where(place == sent, FIRST, 0)
+                    place = place + hits[k]
+
+            return (
+                at + inside.astype(jnp.int32),
+                sent + found,
+                load + (found > 0).astype(jnp.int32),
+            )
+
+        at, sent, load = lax.fori_loop(0, slot_count, step, (at, sent, load))
         for _ in range(MANY):
             for start, end, spare in ((HEAD, at, piece_blocks), (sent_at, sent, 2 * n_row)):
                 entry = base + start + STRIDE * end
@@ -94,12 +110,12 @@
             sent = sent + jnp.where(sent % FEW == 0, 0, 1)
         return at, sent, load
 
-    def lists(base, own_half, meta_own, meta_other, asked_own, asked_other):
+    def lists(base, own_half, meta_own, meta_other):
         for b in range(piece_blocks + 1):
             seen[b] = 0
         ends = (jnp.int32(0),) * 3
         for tile, meta in enumerate((meta_own, meta_other)):
-            ends = scan(base, own_half, meta, asked_own, asked_other, *ends)
+            ends = scan(base, own_half, meta, *ends)
             for i, end in enumerate(ends):
                 out[base + 2 * i + tile] = end
 
@@ -118,10 +134,13 @@
 
     @pl.when(place[1] == 0)
     def _():
-        lists(0, 0, meta_a, meta_b, wanted_a, wanted_b)
+        for k in range(n_row):
+            asked[k] = wanted_a[k, 0]
+            asked[n_row + k] = wanted_b[k, 0]
+        lists(0, 0, meta_a, meta_b)
         copy = pltpu.make_async_copy(out.at[pl.ds(0, size)], own, sems.at[0])
         copy.start()
-        lists(size, 1, meta_b, meta_a, wanted_b, wanted_a)
+        lists(size, 1, meta_b, meta_a)
         handed = pltpu.make_async_copy(out.at[pl.ds(size, size)], other, sems.at[1])
         handed.start()
         copy.wait()
@@ -169,61 +188,76 @@
         put(k).wait()
 
 
-def load_kernel(base, stride, ends, plan, tile_a, tile_b, blocks, sems):
+def fetches(plan, base, stride, ends, tile_a, tile_b, blocks, sems):
     mid, end = plan[ends], plan[ends + 1]
 
     def copy(tile, i):
         slot = plan[base + stride * i]
         return pltpu.make_async_copy(tile.at[slot], blocks.at[i], sems.at[i])
 
-    @pl.loop(0, mid)
+    def start():
+        @pl.loop(0, mid)
+        def _(i):
+            copy(tile_a, i).start()
+
+        @pl.loop(mid, end)
+        def _(i):
+            copy(tile_b, i).start()
+
+    def wait(i):
+        copy(tile_a, i).wait()
+
+    return start, wait
+
+
+def load_kernel(plan, tile_a, array, blocks, held, sems, held_sem):
+    def copy(i):
+        return pltpu.make_async_copy(
+            tile_a.at[plan[HEAD + STRIDE * i]], blocks.at[i], sems.at[i]
+        )
+
+    whole = pltpu.make_async_copy(array, held, held_sem)
+    whole.start()
+
+    @pl.loop(0, plan[0])
     def _(i):
-        copy(tile_a, i).start()
-
-    @pl.loop(mid, end)
+        copy(i).start()
+
+    @pl.loop(0, plan[0])
     def _(i):
-        copy(tile_b, i).start()
-
-    @pl.loop(0, end)
-    def _(i):
-        copy(tile_a, i).wait()
-
-
-def load_both_kernel(base, stride, ends, plan, tile_a, tile_b, array, blocks, held, sems, held_sem):
-    copy = pltpu.make_async_copy(array, held, held_sem)
-    copy.start()
-    load_kernel(base, stride, ends, plan, tile_a, tile_b, blocks, sems)
-    copy.wait()
-
-
-def each_product(plan, base, ends, blocks, pieces, use, then=None):
+        copy(i).wait()
+
+    whole.wait()
+
+
+def each_product(plan, base, ends, block_of, pieces, use, then=None, before=None):
     mid, end = plan[ends], plan[ends + 1]
     unroll = MANY if base == HEAD else FEW
 
-    def run(piece_ref, begin, end):
+    def run(side, begin, end):
         @pl.loop(begin // unroll, end // unroll)
         def _(j):
-            for u in range(unroll):
-                i = unroll * j + u
-                entry = base + STRIDE * i
-                block = blocks[i if base == HEAD else plan[entry]]
-                use(
-                    entry,
-                    jnp.dot(block, piece_ref[plan[entry + 2]], preferred_element_type=jnp.float32),
-                )
+            step = [(unroll * j + u, base + STRIDE * (unroll * j + u)) for u in range(unroll)]
+            if before is not None:
+                for i, entry in step:
+                    before(side, i, entry)
+            for i, entry in step:
+                block = block_of(side, i, entry)
+                piece = pieces[side][plan[entry + 2]]
+                use(entry, jnp.dot(block, piece, preferred_element_type=jnp.float32))
             if then is not None:
-                for u in range(unroll):
-                    then(base + STRIDE * (unroll * j + u))
-
-    run(pieces[0], 0, mid)
-    run(pieces[1], mid, end)
-
-
-def add_products(plan, base, ends, blocks, pieces, total):
+                for i, entry in step:
+                    then(entry)
+
+    run(0, 0, mid)
+    run(1, mid, end)
+
+
+def add_products(plan, base, ends, block_of, pieces, total, before=None):
     def use(entry, value):
         total[plan[entry + 1]] += value
 
-    each_product(plan, base, ends, blocks, pieces, use)
+    each_product(plan, base, ends, block_of, pieces, use, before=before)
 
 
 def split_sides(pieces, vec):
@@ -247,29 +281,27 @@
     sent_at, load_at, plan, tile_a, tile_b, pieces, start, out, blocks, vec, total, held, held_sem, sems
 ):
     n_row = out.shape[0]
-    mid, end = plan[4], plan[5]
-
-    def fetch(tile, i):
-        return pltpu.make_async_copy(tile.at[plan[load_at + i]], blocks.at[i], sems.at[i])
-
-    @pl.loop(0, mid)
-    def _(i):
-        fetch(tile_a, i).start()
-
-    @pl.loop(mid, end)
-    def _(i):
-        fetch(tile_b, i).start()
-
+    begin, wait = fetches(plan, load_at, 1, 4, tile_a, tile_b, blocks, sems)
+    begin()
     copy = pltpu.make_async_copy(start, held, held_sem)
     copy.start()
     split_sides(pieces, vec)
     total[...] = jnp.zeros_like(total)
 
-    @pl.loop(0, end)
-    def _(i):
-        fetch(tile_a, i).wait()
-
-    add_products(plan, sent_at, 2, blocks, (vec.at[0], vec.at[1]), total)
+    def before(side, i, entry):
+        @pl.when(plan[entry + 3] == FIRST)
+        def _():
+            wait(plan[entry])
+
+    add_products(
+        plan,
+        sent_at,
+        2,
+        lambda side, i, entry: blocks[plan[entry]],
+        (vec.at[0], vec.at[1]),
+        total,
+        before,
+    )
     copy.wait()
     for k in range(n_row):
         value = joined(total, k) - center_value * held[k].astype(jnp.float32)
@@ -284,7 +316,14 @@
     copy.start()
     split_sides(pieces, vec)
     total[...] = jnp.zeros_like(total)
-    add_products(plan, sent_at, 2, blocks, (vec.at[0], vec.at[1]), total)
+    add_products(
+        plan,
+        sent_at,
+        2,
+        lambda side, i, entry: blocks[plan[entry]],
+        (vec.at[0], vec.at[1]),
+        total,
+    )
     copy.wait()
 
     def put(k):
@@ -319,11 +358,30 @@
             vec[1, p, :, at : at + width] = jnp.concatenate([two[:, :middle], one[:, middle:]], axis=1)
 
 
-def early_kernel(plan, blocks, q1, q1_other, q2, q2_other, vectors, base, vec, total, own, sem, row_sems):
+def early_kernel(
+    plan,
+    tile_a,
+    tile_b,
+    q1,
+    q1_other,
+    q2,
+    q2_other,
+    vectors,
+    base,
+    vec,
+    total,
+    own,
+    blocks,
+    sem,
+    sems,
+    row_sems,
+):
     width = vectors.shape[1]
     piece_blocks, block_size, _ = base.shape
     copy = pltpu.make_async_copy(vectors, own, sem)
     copy.start()
+    begin, wait = fetches(plan, HEAD, STRIDE, 0, tile_a, tile_b, blocks, sems)
+    begin()
     whole_columns(plan[7], q1, q1_other, vec, 0)
     whole_columns(plan[7], q2, q2_other, vec, width)
     copy.wait()
@@ -340,7 +398,15 @@
         total[b, :, :width] = -center_value * value
         total[b, :, width:] = -value
 
-    add_products(plan, HEAD, 0, blocks, (vec.at[0], vec.at[1]), total)
+    add_products(
+        plan,
+        HEAD,
+        0,
+        lambda side, i, entry: blocks[i],
+        (vec.at[0], vec.at[1]),
+        total,
+        lambda side, i, entry: wait(i),
+    )
 
     @pl.loop(0, piece_blocks)
     def _(b):
@@ -355,8 +421,19 @@
         put(b).wait()
 
 
-def last_kernel(bare_at, plan, blocks, mine, other, base, out, vec, total, own, row_sems):
+def last_kernel(
+    bare_at, plan, blocks, tile_b, mine, other, base, out, vec, total, own, blocks_b, sems, row_sems
+):
     piece_blocks = base.shape[0]
+    mid = plan[0]
+
+    def fetch(i):
+        slot = plan[HEAD + STRIDE * i]
+        return pltpu.make_async_copy(tile_b.at[slot], blocks_b.at[i - mid], sems.at[i - mid])
+
+    @pl.loop(mid, plan[1])
+    def _(i):
+        fetch(i).start()
 
     def put(source, b):
         return pltpu.make_async_copy(source.at[b], out.at[b], row_sems.at[b])
@@ -381,7 +458,14 @@
         def _():
             put(own, plan[entry + 1]).start()
 
-    each_product(plan, HEAD, 0, blocks, (vec.at[0], vec.at[1]), use, then)
+    def block_of(side, i, entry):
+        return blocks[i] if side == 0 else blocks_b[i - mid]
+
+    def before(side, i, entry):
+        if side == 1:
+            fetch(i).wait()
+
+    each_product(plan, HEAD, 0, block_of, (vec.at[0], vec.at[1]), use, then, before)
 
     @pl.loop(0, piece_blocks)
     def _(b):
@@ -475,9 +559,14 @@
     own_list, other_list = call(
         functools.partial(plan_kernel, n_row, piece_blocks, sent_at, load_at, bare_at),
         [((plan_size,), jnp.int32, HBM)] * 2,
-        (place, wanted, wanted_other, meta, meta_other),
+        (place, wanted, after(wanted_other, packed), meta, meta_other),
         (SCALARS,) * 5,
-        [SMEM((2 * plan_size,), jnp.int32), SMEM((piece_blocks + 1,), jnp.int32), DMA((2,))],
+        [
+            SMEM((2 * plan_size,), jnp.int32),
+            SMEM((piece_blocks + 1,), jnp.int32),
+            SMEM((2 * n_row,), jnp.int32),
+            DMA((2,)),
+        ],
         2,
         "plan",
     )
@@ -492,15 +581,16 @@
         "settle",
     )[0]
 
-    def load(base, stride, ends, cue, *array):
-        kernel = load_both_kernel if array else load_kernel
+    def load(cue, array):
         return call(
-            functools.partial(kernel, base, stride, ends),
-            [((capacity, block_size, block_size), jnp.bfloat16, VMEM)]
-            + [(held.shape, held.dtype, VMEM) for held in array],
-            (after(plan, cue), tile, tile_other, *array),
-            (LIST, FAR, ANYWHERE) + (FAR,) * len(array),
-            [DMA((capacity,))] + [DMA] * len(array),
+            load_kernel,
+            [
+                ((capacity // 2, block_size, block_size), jnp.bfloat16, VMEM),
+                (array.shape, array.dtype, VMEM),
+            ],
+            (after(plan, cue), tile, array),
+            (LIST, FAR, FAR),
+            [DMA((capacity // 2,)), DMA],
             2,
             "load",
         )
@@ -552,16 +642,18 @@
         return call(
             early_kernel,
             [(base_shape, jnp.bfloat16, HBM)],
-            (plan, *args),
-            (LIST, HERE, HERE, HERE, HERE, HERE, FAR),
+            (plan, tile, tile_other, *args),
+            (LIST, FAR, ANYWHERE, HERE, HERE, HERE, HERE, FAR),
             [
                 VMEM((2, n_row, block_size, 2 * width), jnp.bfloat16),
                 VMEM((piece_blocks + 1, block_size, 2 * width), jnp.float32),
                 VMEM(vectors.shape, jnp.bfloat16),
+                VMEM((capacity, block_size, block_size), jnp.bfloat16),
                 DMA,
+                DMA((capacity,)),
                 DMA((piece_blocks,)),
             ],
-            18,
+            28,
             "early",
             cost(2 * slot_count, 2 * piece_blocks),
         )[0]
@@ -571,15 +663,17 @@
         (out,) = call(
             functools.partial(last_kernel, bare_at),
             [(base_shape, jnp.bfloat16, HBM)],
-            (plan, blocks, *args),
-            (LIST,) + (HERE,) * 4,
+            (plan, blocks, tile_other, *args),
+            (LIST, HERE, ANYWHERE, HERE, HERE, HERE),
             [
                 VMEM((2, n_row, block_size, width), jnp.bfloat16),
                 VMEM(rows, jnp.float32),
                 VMEM(rows, jnp.bfloat16),
+                VMEM((capacity // 2, block_size, block_size), jnp.bfloat16),
+                DMA((capacity // 2,)),
                 DMA((piece_blocks,)),
             ],
-            9,
+            14,
             "last",
             cost(slot_count, piece_blocks),
         )
@@ -591,11 +685,10 @@
     second_sent = second_blocks(blocks, q2, first_sent, packed)
     q1_other = across(after(q1, second_sent))
     q2_other = across(after(q2, second_sent))
-    (blocks,) = load(HEAD, STRIDE, 0, second_sent)
-    base = early(blocks, q1, q1_other, q2, q2_other, vectors)
+    base = early(q1, q1_other, q2, q2_other, vectors)
     q3 = after(exchange(second_sent), base)
     q3_other = across(q3)
-    blocks, base = load(HEAD, STRIDE, 0, q3, base)
+    blocks, base = load(q3, base)
     return last(blocks, q3, q3_other, base)
 
 

time: 86.9 us -> 86.2 us (level)
  the two profiles are of different devices: /device:TPU:0 before, /device:TPU:13 now
where the time goes in v1:
time: 86.2 us; the launch traced here: 86.6 us
  starting transfers between devices  35.8 us (42%)
  Pallas kernels  26.4 us (31%)
  blocking collectives  13.9 us (16%)
  waiting for transfers between devices  6.79 us (8%)
  other arithmetic  1.61 us (2%)
  local copies, waits for them, and re-layouts  1.37 us (2%)
    pallas_call x9, Pallas kernels, call(): pl.pallas_call(kernel, out_shape=[space(shape, dtype) for shape, dtype, s...  26.4 us
    all_to_all x1, blocking collectives, on_pair(): q2 = exchange(first_sent)  13.9 us
    ppermute x1, starting transfers between devices, on_pair(): across(after(other_list, packed))  10.7 us
    ppermute x1, starting transfers between devices, on_pair(): q1_other = across(after(q1, second_sent))  6.78 us
    all_to_all x1, starting transfers between devices, on_pair(): exchange(jnp.broadcast_to(needed, (n_row, LANES)))  5.69 us
    all_to_all x1, starting transfers between devices, on_pair(): q1 = exchange(after(packed, own_list))  4.62 us
    all_to_all x1, starting transfers between devices, on_pair(): q3 = after(exchange(second_sent), base)  4.03 us
  transfers between devices with their start and end apart: 11, of which 6 were waited for; matrix products, arithmetic and copies ran while one was open for 3% of the time, Pallas kernels for 18%

profile of v1, /device:TPU:13, one launch (start us, length us, event | category | flops | bytes accessed | tf_op | source)
XLA Modules:
  0.0 86.6 jit_solution(15278225373447000799)
XLA Ops:
  2.1 5.7 %all-to-all-start = ((s32[8,1,128]{2,1,0:T(1,128)}), s32[8,1,128]{2,1,0:T(1,128)S(1)}, u32[]{:S(2)}, u32[]{:S(2)}) async-start(s32[8,1,128]{2,1,0:T(1,128)} %broadcast_in_dim.21), calls=%async_computation | async-start | bytes 8192 | tf_op jit(solution)/shard_map/all_to_all | solution.py:530
  8.5 0.7 pad_add_fusion.1.meta_a
  9.9 0.7 collective-permute-done.meta_b
  10.6 1.3 %all-to-all-done = s32[8,1,128]{2,1,0:T(1,128)S(1)} async-done(((s32[8,1,128]{2,1,0:T(1,128)}), s32[8,1,128]{2,1,0:T(1,128)S(1)}, u32[]{:S(2)}, u32[]{:S(2)}) %all-to-all-start) | async-done | bytes 4128 | tf_op jit(solution)/shard_map/all_to_all | solution.py:530
  11.9 1.7 %pick.1.picked = bf16[8,256,128]{2,1,0:T(8,128)(2,1)S(1)} custom-call(s32[8,128]{1,0:T(8,128)S(1)} %bitcast.15, bf16[8192,128]{1,0:T(8,128)(2,1)} %vectors.3), custom_call_target="tpu_custom_call" | custom-call | tf_op jit(solution)/shard_map/pick/pallas_call | solution.py:484
  13.6 1.5 %collective-permute-start.2 = (bf16[8,256,128]{2,1,0:T(8,128)(2,1)S(1)}, bf16[8,256,128]{2,1,0:T(8,128)(2,1)S(1)}, u32[]{:S(2)}, u32[]{:S(2)}) collective-permute-start(bf16[8,256,128]{2,1,0:T(8,128)(2,1)S(1)} %pick.1.picked), channel_id=1, source_target_pairs={{0,2},{2,0},{1,3},{3,1},{4,6},{6,4},{5,7},{7,5},{8,10},{10,8},{9,1... | collective-permute-start | bytes 1572872 | tf_op jit(solution)/shard_map/ppermute | solution.py:542
  15.2 1.5 %collective-permute-done.2.picked_b = bf16[8,256,128]{2,1,0:T(8,128)(2,1)S(1)} collective-permute-done((bf16[8,256,128]{2,1,0:T(8,128)(2,1)S(1)}, bf16[8,256,128]{2,1,0:T(8,128)(2,1)S(1)}, u32[]{:S(2)}, u32[]{:S(2)}) %collective-permute-start.2) | collective-permute-done | bytes 524320 | tf_op jit(solution)/shard_map/ppermute | solution.py:542
  16.6 1.5 %pack.1.start.previous = bf16[8,256,128]{2,1,0:T(8,128)(2,1)} custom-call(s32[2]{0:T(128)S(1)} %pad_add_fusion.place, bf16[8,256,128]{2,1,0:T(8,128)(2,1)S(1)} %pick.1.picked, bf16[8,256,128]{2,1,0:T(8,128)(2,1)S(1)} %collective-permute-done.2.picked_b), custom_call_target="tpu_custom_call" | custom-call | tf_op jit(solution)/shard_map/pack/pallas_call | solution.py:484
  18.1 0.7 plan.1
  18.9 4.6 %all-to-all-start.1 = ((bf16[8,256,128]{2,1,0:T(8,128)(2,1)}), bf16[8,256,128]{2,1,0:T(8,128)(2,1)S(1)}, u32[]{:S(2)}, u32[]{:S(2)}) async-start(bf16[8,256,128]{2,1,0:T(8,128)(2,1)} %pack.1.start.previous), calls=%async_computation.1 | async-start | bytes 1048576 | tf_op jit(solution)/shard_map/all_to_all | solution.py:573
  23.5 10.7 %collective-permute-start.3 = (s32[2048]{0:T(1024)}, s32[2048]{0:T(1024)S(1)}, u32[]{:S(2)}, u32[]{:S(2)}) collective-permute-start(s32[2048]{0:T(1024)} %get-tuple-element.26), channel_id=1, source_target_pairs={{0,2},{2,0},{1,3},{3,1},{4,6},{6,4},{5,7},{7,5},{8,10},{10,8},{9,1... | collective-permute-start | bytes 24584 | tf_op jit(solution)/shard_map/ppermute | solution.py:577
  34.2 1.0 %collective-permute-done.3.handed = s32[2048]{0:T(1024)S(1)} collective-permute-done((s32[2048]{0:T(1024)}, s32[2048]{0:T(1024)S(1)}, u32[]{:S(2)}, u32[]{:S(2)}) %collective-permute-start.3) | collective-permute-done | bytes 8224 | tf_op jit(solution)/shard_map/ppermute | solution.py:577
  35.9 1.2 %settle.1.plan = s32[2048]{0:T(1024)S(4)} custom-call(s32[2]{0:T(128)S(1)} %pad_add_fusion.place, s32[2048]{0:T(1024)S(1)} %copy-done, s32[2048]{0:T(1024)S(1)} %collective-permute-done.3.handed), custom_call_target="tpu_custom_call" | custom-call | tf_op jit(solution)/shard_map/settle/pallas_call | solution.py:484
  37.2 3.4 %sent.2 = (bf16[8,256,128]{2,1,0:T(8,128)(2,1)S(1)}, bf16[64,256,256]{2,1,0:T(8,128)(2,1)S(1)}) custom-call(s32[2048]{0:T(1024)S(4)} %settle.1.plan, bf16[32,256,256]{2,1,0:T(8,128)(2,1)} %bitcast.19, bf16[32,256,256]{2,1,0:T(8,128)(2,1)} %collective-permute-done.4.tile_b, bf16[8,256,128]{2,1,0:T(8,128)(2,1)S(1)} %all-to-all-done.1.pieces.q1, ...), custom_call_target="tpu_custom_call" | custom-call | flops 134217728 | bytes 2621440 | tf_op jit(solution)/shard_map/sent/pallas_call | solution.py:484
  40.5 13.9 %all_to_all.24.pieces.q2 = bf16[8,256,128]{2,1,0:T(8,128)(2,1)S(1)} all-to-all(bf16[8,256,128]{2,1,0:T(8,128)(2,1)S(1)} %get-tuple-element.30.current), channel_id=1, replica_groups=mesh['row'=8,'col'=2,'vec'=2] {'row'}, dimensions={0} | all-to-all | bytes 1048576 | tf_op jit(solution)/shard_map/all_to_all | solution.py:684
  54.4 2.5 %sent.3 = bf16[8,256,128]{2,1,0:T(8,128)(2,1)} custom-call(s32[2048]{0:T(1024)S(4)} %settle.1.plan, bf16[64,256,256]{2,1,0:T(8,128)(2,1)S(1)} %get-tuple-element.29.blocks, bf16[8,256,128]{2,1,0:T(8,128)(2,1)S(1)} %all_to_all.24.pieces.q2, bf16[8,256,128]{2,1,0:T(8,128)(2,1)S(1)} %get-tuple-element.30.current, bf16[8,256,128]{2,1,0:T(8,128)(2,1)} %pack.1.start.previous), custom_call_target="tpu_custom_call" | custom-call | flops 134217728 | bytes 2621440 | tf_op jit(solution)/shard_map/sent/pallas_call | solution.py:484
  56.9 4.0 %all-to-all-start.3 = ((bf16[8,256,128]{2,1,0:T(8,128)(2,1)}), bf16[8,256,128]{2,1,0:T(8,128)(2,1)S(1)}, u32[]{:S(2)}, u32[]{:S(2)}) async-start(bf16[8,256,128]{2,1,0:T(8,128)(2,1)} %sent.3), calls=%async_computation.3 | async-start | bytes 1048576 | tf_op jit(solution)/shard_map/all_to_all | solution.py:689
  60.9 6.8 %collective-permute-start.5 = (bf16[8,256,128]{2,1,0:T(8,128)(2,1)S(1)}, bf16[8,256,128]{2,1,0:T(8,128)(2,1)S(1)}, u32[]{:S(2)}, u32[]{:S(2)}) collective-permute-start(bf16[8,256,128]{2,1,0:T(8,128)(2,1)S(1)} %all-to-all-done.1.pieces.q1), channel_id=1, source_target_pairs={{0,2},{2,0},{1,3},{3,1},{4,6},{6,4},{5,7},{7,5},{8,10},{10,8},{9,1... | collective-permute-start | bytes 1572872 | tf_op jit(solution)/shard_map/ppermute | solution.py:686
  67.7 1.5 %collective-permute-done.5.q1_other = bf16[8,256,128]{2,1,0:T(8,128)(2,1)S(1)} collective-permute-done((bf16[8,256,128]{2,1,0:T(8,128)(2,1)S(1)}, bf16[8,256,128]{2,1,0:T(8,128)(2,1)S(1)}, u32[]{:S(2)}, u32[]{:S(2)}) %collective-permute-start.5) | collective-permute-done | bytes 524320 | tf_op jit(solution)/shard_map/ppermute | solution.py:686
  69.2 0.7 collective-permute-done.6.q2_other
  70.0 8.1 %early.1.array = bf16[32,256,128]{2,1,0:T(8,128)(2,1)} custom-call(s32[2048]{0:T(1024)S(4)} %settle.1.plan, bf16[32,256,256]{2,1,0:T(8,128)(2,1)} %bitcast.20, bf16[32,256,256]{2,1,0:T(8,128)(2,1)} %collective-permute-done.4.tile_b, bf16[8,256,128]{2,1,0:T(8,128)(2,1)S(1)} %all-to-all-done.1.pieces.q1, ...), custom_call_target="tpu_custom_call" | custom-call | flops 1073741824 | bytes 20971520 | tf_op jit(solution)/shard_map/early/pallas_call | solution.py:484
  78.1 1.2 %collective-permute-start.7 = (bf16[8,256,128]{2,1,0:T(8,128)(2,1)S(1)}, bf16[8,256,128]{2,1,0:T(8,128)(2,1)S(1)}, u32[]{:S(2)}, u32[]{:S(2)}) collective-permute-start(bf16[8,256,128]{2,1,0:T(8,128)(2,1)S(1)} %all-to-all-done.3.mine), channel_id=1, source_target_pairs={{0,2},{2,0},{1,3},{3,1},{4,6},{6,4},{5,7},{7,5},{8,10},{10,8},{9,1... | collective-permute-start | bytes 1572872 | tf_op jit(solution)/shard_map/ppermute | solution.py:690
  79.3 2.4 %load.1 = (bf16[32,256,256]{2,1,0:T(8,128)(2,1)S(1)}, bf16[32,256,128]{2,1,0:T(8,128)(2,1)S(1)}) custom-call(s32[2048]{0:T(1024)S(4)} %settle.1.plan, bf16[32,256,256]{2,1,0:T(8,128)(2,1)} %bitcast.21, bf16[32,256,128]{2,1,0:T(8,128)(2,1)} %early.1.array), custom_call_target="tpu_custom_call" | custom-call | tf_op jit(solution)/shard_map/load/pallas_call | solution.py:484
  81.7 4.9 %last.1 = bf16[32,256,128]{2,1,0:T(8,128)(2,1)} custom-call(s32[2048]{0:T(1024)S(4)} %settle.1.plan, bf16[32,256,256]{2,1,0:T(8,128)(2,1)S(1)} %get-tuple-element.35.blocks, bf16[32,256,256]{2,1,0:T(8,128)(2,1)} %collective-permute-done.4.tile_b, bf16[8,256,128]{2,1,0:T(8,128)(2,1)S(1)} %all-to-all-done.3.mine, ...), custom_call_target="tpu_custom_call" | custom-call | flops 536870912 | bytes 10485760 | tf_op jit(solution)/shard_map/last/pallas_call | solution.py:484
  (15 shorter events, 3.6 us)
Async XLA Ops:
  0.0 37.1 %collective-permute-start.4 = (bf16[32,256,256]{2,1,0:T(8,128)(2,1)}, bf16[32,256,256]{2,1,0:T(8,128)(2,1)}, u32[]{:S(2)}, u32[]{:S(2)}) collective-permute-start(bf16[32,256,256]{2,1,0:T(8,128)(2,1)} %bitcast.18), channel_id=1, source_target_pairs={{0,2},{2,0},{1,3},{3,1},{4,6},{6,4},{5,7},{7,5},{8,10},{10,8},{9,1... | collective-permute-start | bytes 12582920 | tf_op jit(solution)/shard_map/ppermute | solution.py:541
  2.1 9.7 %all-to-all-start = ((s32[8,1,128]{2,1,0:T(1,128)}), s32[8,1,128]{2,1,0:T(1,128)S(1)}, u32[]{:S(2)}, u32[]{:S(2)}) async-start(s32[8,1,128]{2,1,0:T(1,128)} %broadcast_in_dim.21), calls=%async_computation | async-start | bytes 8192 | tf_op jit(solution)/shard_map/all_to_all | solution.py:530
  9.2 1.4 %collective-permute-start = (s32[65]{0:T(128)S(1)}, s32[65]{0:T(128)S(1)}, u32[]{:S(2)}, u32[]{:S(2)}) collective-permute-start(s32[65]{0:T(128)S(1)} %pad_add_fusion.1.meta_a), channel_id=1, source_target_pairs={{0,2},{2,0},{1,3},{3,1},{4,6},{6,4},{5,7},{7,5},{8,10},{10,8},{9,1... | collective-permute-start | bytes 788 | tf_op jit(solution)/shard_map/ppermute | solution.py:529
  13.6 3.0 %collective-permute-start.2 = (bf16[8,256,128]{2,1,0:T(8,128)(2,1)S(1)}, bf16[8,256,128]{2,1,0:T(8,128)(2,1)S(1)}, u32[]{:S(2)}, u32[]{:S(2)}) collective-permute-start(bf16[8,256,128]{2,1,0:T(8,128)(2,1)S(1)} %pick.1.picked), channel_id=1, source_target_pairs={{0,2},{2,0},{1,3},{3,1},{4,6},{6,4},{5,7},{7,5},{8,10},{10,8},{9,1... | collective-permute-start | bytes 1572872 | tf_op jit(solution)/shard_map/ppermute | solution.py:542
  15.1 3.0 %collective-permute-start.1 = (s32[8,128]{1,0:T(8,128)S(1)}, s32[8,128]{1,0:T(8,128)S(1)}, u32[]{:S(2)}, u32[]{:S(2)}) collective-permute-start(s32[8,128]{1,0:T(8,128)S(1)} %bitcast.16), channel_id=1, source_target_pairs={{0,2},{2,0},{1,3},{3,1},{4,6},{6,4},{5,7},{7,5},{8,10},{10,8},{9,1... | collective-permute-start | bytes 12296 | tf_op jit(solution)/shard_map/ppermute | solution.py:543
  18.9 18.3 %all-to-all-start.1 = ((bf16[8,256,128]{2,1,0:T(8,128)(2,1)}), bf16[8,256,128]{2,1,0:T(8,128)(2,1)S(1)}, u32[]{:S(2)}, u32[]{:S(2)}) async-start(bf16[8,256,128]{2,1,0:T(8,128)(2,1)} %pack.1.start.previous), calls=%async_computation.1 | async-start | bytes 1048576 | tf_op jit(solution)/shard_map/all_to_all | solution.py:573
  23.5 11.7 %collective-permute-start.3 = (s32[2048]{0:T(1024)}, s32[2048]{0:T(1024)S(1)}, u32[]{:S(2)}, u32[]{:S(2)}) collective-permute-start(s32[2048]{0:T(1024)} %get-tuple-element.26), channel_id=1, source_target_pairs={{0,2},{2,0},{1,3},{3,1},{4,6},{6,4},{5,7},{7,5},{8,10},{10,8},{9,1... | collective-permute-start | bytes 24584 | tf_op jit(solution)/shard_map/ppermute | solution.py:577
  35.2 0.7 copy-start
  56.9 21.2 %all-to-all-start.3 = ((bf16[8,256,128]{2,1,0:T(8,128)(2,1)}), bf16[8,256,128]{2,1,0:T(8,128)(2,1)S(1)}, u32[]{:S(2)}, u32[]{:S(2)}) async-start(bf16[8,256,128]{2,1,0:T(8,128)(2,1)} %sent.3), calls=%async_computation.3 | async-start | bytes 1048576 | tf_op jit(solution)/shard_map/all_to_all | solution.py:689
  60.9 8.3 %collective-permute-start.5 = (bf16[8,256,128]{2,1,0:T(8,128)(2,1)S(1)}, bf16[8,256,128]{2,1,0:T(8,128)(2,1)S(1)}, u32[]{:S(2)}, u32[]{:S(2)}) collective-permute-start(bf16[8,256,128]{2,1,0:T(8,128)(2,1)S(1)} %all-to-all-done.1.pieces.q1), channel_id=1, source_target_pairs={{0,2},{2,0},{1,3},{3,1},{4,6},{6,4},{5,7},{7,5},{8,10},{10,8},{9,1... | collective-permute-start | bytes 1572872 | tf_op jit(solution)/shard_map/ppermute | solution.py:686
  67.7 2.3 %collective-permute-start.6 = (bf16[8,256,128]{2,1,0:T(8,128)(2,1)S(1)}, bf16[8,256,128]{2,1,0:T(8,128)(2,1)S(1)}, u32[]{:S(2)}, u32[]{:S(2)}) collective-permute-start(bf16[8,256,128]{2,1,0:T(8,128)(2,1)S(1)} %all_to_all.24.pieces.q2), channel_id=1, source_target_pairs={{0,2},{2,0},{1,3},{3,1},{4,6},{6,4},{5,7},{7,5},{8,10},{10,8},{9,1... | collective-permute-start | bytes 1572872 | tf_op jit(solution)/shard_map/ppermute | solution.py:687
  78.1 3.6 %collective-permute-start.7 = (bf16[8,256,128]{2,1,0:T(8,128)(2,1)S(1)}, bf16[8,256,128]{2,1,0:T(8,128)(2,1)S(1)}, u32[]{:S(2)}, u32[]{:S(2)}) collective-permute-start(bf16[8,256,128]{2,1,0:T(8,128)(2,1)S(1)} %all-to-all-done.3.mine), channel_id=1, source_target_pairs={{0,2},{2,0},{1,3},{3,1},{4,6},{6,4},{5,7},{7,5},{8,10},{10,8},{9,1... | collective-permute-start | bytes 1572872 | tf_op jit(solution)/shard_map/ppermute | solution.py:690
